TPU v7x, 512 devices: a whole 4x8x8 slice. The times are simulated.
512 devices in a mesh: tm: 32 (over z, y_lo, core), freq: 16 (over x, y_hi).
Axes of the slice: x: 4, y: 8 (y_hi: 4, y_lo: 2; y = y_hi * 2 + y_lo), z: 8, core: 2. Of those that a mesh axis runs over, the one named last changes fastest.
Arguments:
- jones_gains: bfloat16 [1024, 256, 8, 128], P('tm', 'freq'), may hold values from -6 to 6
- right_terms: bfloat16 [1024, 256, 8, 128], P('tm', 'freq'), may hold values from -6 to 6
- normal_diagonal: bfloat16 [1024, 256, 2, 128], P('tm', 'freq'), may hold values from 0.5 to 2
- normal_cross: bfloat16 [1024, 256, 2, 128], P('tm', 'freq'), may hold values from -0.5 to 0.5
- station_flags: int32 [1024, 256, 64], P('tm', 'freq'), may hold values 0 or 1
- time_weights: bfloat16 [1024, 1024], P('tm'), may hold values from -1 to 2
- time_kernel: bfloat16 [1024, 1024], P('tm'), may hold values from -1 to 2
- channel_weights: bfloat16 [256, 256], P('freq'), may hold values from -1 to 2
- channel_kernel: bfloat16 [256, 256], P('freq'), may hold values from -1 to 2
Outputs:
- smoothed_gains: float32 [1024, 256, 8, 128], P('tm', 'freq')
All inputs are finite; a program needn't handle non-finite values. No bound on the sum of `station_flags` on one device may be relied on, other than what follows from the above.
Results may differ from a plain program's by a relative error of at most 0.0054.
Values may be sent and summed in bfloat16 or wider, within the bound.
A program may use at most 64 MiB of HBM per device.

v0:
```python
import jax
import jax.numpy as jnp
from jax import lax
from jax.sharding import PartitionSpec as P

DIRS = 2


def product_terms(right_terms, normal_diagonal, normal_cross):
    upper_left = normal_diagonal[:, :, 0]
    lower_right = normal_diagonal[:, :, 1]
    cross_real = normal_cross[:, :, 0]
    cross_imag = normal_cross[:, :, 1]
    entries = []
    for offset in (0, 4):
        lead_real = right_terms[:, :, offset]
        lead_imag = right_terms[:, :, offset + 1]
        tail_real = right_terms[:, :, offset + 2]
        tail_imag = right_terms[:, :, offset + 3]
        left_real = lead_real * upper_left + tail_real * cross_real + tail_imag * cross_imag
        left_imag = lead_imag * upper_left + tail_imag * cross_real - tail_real * cross_imag
        right_real = lead_real * cross_real - lead_imag * cross_imag + tail_real * lower_right
        right_imag = lead_real * cross_imag + lead_imag * cross_real + tail_imag * lower_right
        entries += [left_real, left_imag, right_real, right_imag]
    return jnp.stack(entries, axis=2)


def updated_gains(jones_gains, right_terms, normal_diagonal, normal_cross, station_flags):
    previous = jones_gains.astype(jnp.float32)
    product = product_terms(
        right_terms.astype(jnp.float32),
        normal_diagonal.astype(jnp.float32),
        normal_cross.astype(jnp.float32),
    )
    flags_wide = jnp.tile(station_flags, (1, 1, DIRS))[:, :, None, :]
    return jnp.where(flags_wide == 1, previous, 0.5 * previous + 0.5 * product).astype(jnp.bfloat16)


def apply_times(source, rows_block):
    return jnp.dot(rows_block, source, preferred_element_type=jnp.float32)


def contract_channels(source):

    def apply_rows(rows_block, first_row):
        return jnp.einsum("gf,rfc->rgc", rows_block, source, preferred_element_type=jnp.float32)

    return apply_rows


def apply_channels(data, weight_rows, kernel_rows, maker):
    channel_mixed = maker(data)(
        lax.all_gather(weight_rows, "freq", axis=0, tiled=True), jnp.int32(0)
    ).astype(jnp.bfloat16)
    return maker(channel_mixed)(
        lax.all_gather(kernel_rows, "freq", axis=0, tiled=True), jnp.int32(0)
    )


def body(
    jones_gains,
    right_terms,
    normal_diagonal,
    normal_cross,
    station_flags,
    time_weights,
    time_kernel,
    channel_weights,
    channel_kernel,
):
    updated = updated_gains(jones_gains, right_terms, normal_diagonal, normal_cross, station_flags)
    local_times, local_channels, components, columns = updated.shape
    time_groups = lax.axis_size("tm")
    channel_groups = lax.axis_size("freq")
    slab_width = components * columns // time_groups
    sub_times = local_times // channel_groups
    sliced = updated.reshape(local_times, local_channels, time_groups, slab_width)
    exchanged = lax.all_to_all(sliced, "tm", split_axis=2, concat_axis=0, tiled=True)
    total_times = exchanged.shape[0]
    time_major = exchanged.reshape(total_times, local_channels * slab_width)
    time_mixed = apply_times(
        time_major, lax.all_gather(time_weights, "tm", axis=0, tiled=True)
    ).astype(jnp.bfloat16)
    time_smooth = apply_times(
        time_mixed, lax.all_gather(time_kernel, "tm", axis=0, tiled=True)
    ).astype(jnp.bfloat16)
    returned = lax.all_to_all(
        time_smooth.reshape(total_times, local_channels, 1, slab_width),
        "tm",
        split_axis=0,
        concat_axis=2,
        tiled=True,
    )
    regrouped = returned.reshape(channel_groups, sub_times, local_channels, components * columns)
    channel_major = lax.all_to_all(regrouped, "freq", split_axis=0, concat_axis=2, tiled=True)
    smoothed = apply_channels(
        channel_major.reshape(sub_times, -1, components * columns),
        channel_weights,
        channel_kernel,
        contract_channels,
    )
    restored = lax.all_to_all(
        smoothed.reshape(1, sub_times, -1, components * columns),
        "freq",
        split_axis=2,
        concat_axis=0,
        tiled=True,
    )
    return restored.reshape(local_times, local_channels, components, columns)


def solution(mesh):
    in_specs = (
        P("tm", "freq", None, None),
        P("tm", "freq", None, None),
        P("tm", "freq", None, None),
        P("tm", "freq", None, None),
        P("tm", "freq", None),
        P("tm", None),
        P("tm", None),
        P("freq", None),
        P("freq", None),
    )
    out_specs = P("tm", "freq", None, None)
    return jax.shard_map(body, mesh=mesh, in_specs=in_specs, out_specs=out_specs, check_vma=False)
```

profile of v0, /device:TPU:8, one launch (start us, length us, event | category | flops | bytes accessed | tf_op | source)
XLA Modules:
  0.0 428.3 jit_solution(6705056181367100142)
XLA Ops:
  6.5 0.0 copy-start
  6.5 0.0 copy-start.1
  6.5 0.0 all-gather.3.cloned.1.call-start
  6.5 0.7 all-gather.3.cloned.1.call-update
  7.3 0.0 all-gather.5.cloned.1.call-start
  7.3 0.7 all-gather.5.cloned.1.call-update
  8.0 0.0 copy-start.2
  8.0 1.5 convert_element_type.32
  9.5 0.0 copy-done
  9.5 0.3 convert_element_type.33
  9.8 0.0 copy-done.1
  9.8 0.3 convert_element_type.34
  10.1 0.0 copy-done.2
  10.2 0.3 tile.2
  10.4 0.2 eq.17
  10.7 3.0 multiply_add_fusion
  13.6 2.2 multiply_add_fusion.3
  15.8 2.8 multiply_add_fusion.1
  18.6 5.4 %stack.2 = f32[32,16,8,128]{3,2,1,0:T(8,128)S(1)} concatenate(f32[32,16,1,128]{3,2,1,0:T(1,128)} %get-tuple-element.10, f32[32,16,1,128]{3,2,1,0:T(1,128)} %get-tuple-element.9, f32[32,16,1,128]{3,2,1,0:T(1,128)} %get-tuple-element.12, f32[32,16,1,128]{3,2,1,0:T(1,128)} %get-tuple-element.11, f32[32,16,1,128]{3,2,1,0:T(1,128)} %get-tuple-element.7, ...), dimensions={2} | concatenate | bytes 4194304 | tf_op jit(solution)/shard_map/stack | solution.py:25
  24.0 1.7 fusion.1
  25.7 3.3 reshape.40
  29.0 5.8 %copy.33 = bf16[32,16,32,32]{3,1,0,2:T(8,128)(2,1)} copy(bf16[32,16,32,32]{3,2,1,0:T(8,128)(2,1)} %reshape.40) | data formatting | bytes 2097152 | tf_op jit(solution)/shard_map/reshape | solution.py:77
  34.7 6.7 %reshape.49 = bf16[32,2,8192]{2,1,0:T(2,128)(2,1)S(1)} reshape(bf16[32,32,16,32]{3,2,1,0:T(8,128)(2,1)} %bitcast.59) | data formatting | bytes 2097152
  41.4 43.6 %all_to_all.60 = bf16[32,2,8192]{2,1,0:T(2,128)(2,1)S(1)} all-to-all(bf16[32,2,8192]{2,1,0:T(2,128)(2,1)S(1)} %reshape.49), channel_id=1, replica_groups=mesh['tm'=32,'freq'=16] {'tm'}, dimensions={0} | all-to-all | bytes 2097152 | tf_op jit(solution)/shard_map/all_to_all | solution.py:78
  85.1 3.5 reshape.50
  88.6 5.3 %bitcast_bitcast_fusion = bf16[32,32,16,1,32]{4,2,1,0,3:T(8,128)(2,1)} fusion(bf16[32,32,16,32]{3,2,1,0:T(8,128)(2,1)} %reshape.50), kind=kLoop, calls=%fused_computation.20 | loop fusion | bytes 2097152 | tf_op jit(solution)/shard_map/all_to_all | solution.py:78
  93.9 5.9 %reshape.41 = bf16[1024,512]{1,0:T(8,128)(2,1)S(1)} reshape(bf16[32,32,16,1,32]{4,2,1,0,3:T(8,128)(2,1)} %bitcast_bitcast_fusion) | data formatting | bytes 2097152 | tf_op jit(solution)/shard_map/reshape | solution.py:80
  99.9 0.0 all-gather.3.cloned.1.call-done
  99.9 63.6 %all-gather.5.cloned.1.call-done = bf16[1024,1024]{1,0:T(8,128)(2,1)} async-done(((bf16[32,1024]{1,0:T(8,128)(2,1)}), bf16[1024,1024]{1,0:T(8,128)(2,1)}) %all-gather.5.cloned.1.call-update) | async-done | bytes 2097168 | tf_op jit(solution)/shard_map/all_gather | solution.py:85
  163.5 4.6 %convolution_convert_fusion.1 = bf16[512,1024]{1,0:T(8,128)(2,1)S(1)} fusion(bf16[1024,1024]{1,0:T(8,128)(2,1)} %all-gather.5.cloned.1.call-done, bf16[1024,512]{1,0:T(8,128)(2,1)S(1)} %reshape.41, bf16[1024,1024]{1,0:T(8,128)(2,1)} %all-gather.3.cloned.1.call-done), kind=kOutput, calls=%fused_computation.6 | convolution fusion | flops 2148532224 | bytes 6291456 | tf_op jit(solution)/shard_map/dot_general | solution.py:40
  168.1 4.8 %copy.21 = bf16[1024,16,1,32]{3,1,2,0:T(8,128)(2,1)} copy(bf16[1024,16,1,32]{0,3,1,2:T(8,128)(2,1)S(1)} %bitcast.66) | data formatting | bytes 2097152 | tf_op jit(solution)/shard_map/reshape | solution.py:88
  172.9 6.7 %reshape.51 = bf16[32,2,8192]{2,1,0:T(2,128)(2,1)S(1)} reshape(bf16[1024,1,16,32]{3,2,1,0:T(8,128)(2,1)} %bitcast.58) | data formatting | bytes 2097152
  179.5 36.2 %all_to_all.61 = bf16[32,2,8192]{2,1,0:T(2,128)(2,1)S(1)} all-to-all(bf16[32,2,8192]{2,1,0:T(2,128)(2,1)S(1)} %reshape.51), channel_id=1, replica_groups=mesh['tm'=32,'freq'=16] {'tm'}, dimensions={0} | all-to-all | bytes 2097152 | tf_op jit(solution)/shard_map/all_to_all | solution.py:87
  215.7 3.5 reshape.52
  219.3 8.2 %copy.30 = bf16[32,32,16,1,32]{1,0,4,2,3:T(8,128)(2,1)} copy(bf16[32,32,16,1,32]{4,2,1,0,3:T(8,128)(2,1)} %bitcast.60) | data formatting | bytes 2097152 | tf_op jit(solution)/shard_map/all_to_all | solution.py:87
  227.4 10.8 %copy.23 = bf16[32,16,32,1,32]{4,2,1,0,3:T(8,128)(2,1)} copy(bf16[32,16,32,1,32]{0,2,4,1,3:T(8,128)(2,1)} %bitcast.61) | data formatting | bytes 2097152 | tf_op jit(solution)/shard_map/all_to_all | solution.py:87
  238.3 7.0 %reshape.43 = bf16[16,2,16,1024]{3,2,1,0:T(8,128)(2,1)} reshape(bf16[32,16,32,1,32]{4,2,1,0,3:T(8,128)(2,1)} %copy.23) | data formatting | bytes 2097152 | tf_op jit(solution)/shard_map/reshape | solution.py:94
  245.3 0.0 copy-start.3
  245.3 0.0 copy-start.4
  245.3 8.9 %all-to-all-start.2 = ((bf16[16,2,16,1024]{3,2,1,0:T(8,128)(2,1)}), bf16[16,2,16,1024]{3,2,1,0:T(8,128)(2,1)S(1)}, u32[]{:S(2)}, u32[]{:S(2)}) async-start(bf16[16,2,16,1024]{3,2,1,0:T(8,128)(2,1)} %reshape.43), calls=%async_computation.2 | async-start | bytes 2097152 | tf_op jit(solution)/shard_map/all_to_all | solution.py:95
  254.2 0.0 copy-done.3
  254.2 61.3 %all_gather.14 = bf16[256,256]{1,0:T(8,128)(2,1)S(1)} all-gather(bf16[16,256]{1,0:T(8,128)(2,1)S(1)} %copy-done.3), channel_id=1, replica_groups=mesh['tm'=32,'freq'=16] {'freq'}, dimensions={0}, use_global_device_ids=true | all-gather | bytes 139264 | tf_op jit(solution)/shard_map/all_gather | solution.py:53
  315.4 0.0 copy-done.4
  315.5 69.7 %all_gather.15 = bf16[256,256]{1,0:T(8,128)(2,1)S(1)} all-gather(bf16[16,256]{1,0:T(8,128)(2,1)S(1)} %copy-done.4), channel_id=1, replica_groups=mesh['tm'=32,'freq'=16] {'freq'}, dimensions={0}, use_global_device_ids=true | all-gather | bytes 139264 | tf_op jit(solution)/shard_map/all_gather | solution.py:56
  385.2 0.0 all-to-all-done.2
  385.2 0.1 copy.24
  385.3 0.8 convolution_bitcast_fusion
  386.2 2.3 copy.26
  388.5 30.2 %all_to_all.62 = f32[1,2,256,1024]{3,1,0,2:T(2,128)S(1)} all-to-all(f32[1,2,256,1024]{3,1,0,2:T(2,128)} %copy.26), channel_id=1, replica_groups=mesh['tm'=32,'freq'=16] {'freq'}, dimensions={2} | all-to-all | bytes 4194304 | tf_op jit(solution)/shard_map/all_to_all | solution.py:102
  418.7 0.7 copy.27
  419.4 0.2 copy.28
  419.6 1.8 copy.31
  (1 shorter events, 0.0 us)
Async XLA Ops:
  6.5 3.0 copy-start
  6.5 3.3 copy-start.1
  6.5 93.3 %all-gather.3.cloned.1.call-start = ((), (), s32[]{:S(2)}) async-start(), calls=%async_computation.4 | async-start | bytes 2162688 | tf_op jit(solution)/shard_map/all_gather | solution.py:82
  7.3 156.2 %all-gather.5.cloned.1.call-start = ((), (), s32[]{:S(2)}) async-start(), calls=%async_computation.5 | async-start | bytes 2162688 | tf_op jit(solution)/shard_map/all_gather | solution.py:85
  8.0 2.1 copy-start.2
  245.3 8.9 %copy-start.3 = (bf16[16,256]{1,0:T(8,128)(2,1)S(1)}, bf16[16,256]{1,0:T(8,128)(2,1)}, u32[]{:S(2)}) copy-start(bf16[16,256]{1,0:T(8,128)(2,1)} %param.16) | copy-start | bytes 24580
  245.3 70.2 %copy-start.4 = (bf16[16,256]{1,0:T(8,128)(2,1)S(1)}, bf16[16,256]{1,0:T(8,128)(2,1)}, u32[]{:S(2)}) copy-start(bf16[16,256]{1,0:T(8,128)(2,1)} %param.17) | copy-start | bytes 24580
  245.3 139.9 %all-to-all-start.2 = ((bf16[16,2,16,1024]{3,2,1,0:T(8,128)(2,1)}), bf16[16,2,16,1024]{3,2,1,0:T(8,128)(2,1)S(1)}, u32[]{:S(2)}, u32[]{:S(2)}) async-start(bf16[16,2,16,1024]{3,2,1,0:T(8,128)(2,1)} %reshape.43), calls=%async_computation.2 | async-start | bytes 2097152 | tf_op jit(solution)/shard_map/all_to_all | solution.py:95
Sparse Core Ops, SparseCore 0:
  9.5 84.7 all-gather.2
  96.5 66.9 all-gather.4
where the time goes:
time: 430 us; the launch traced here: 428 us
  blocking collectives  241 us (56%)
  local copies, waits for them, and re-layouts  82.5 us (19%)
  waiting for transfers between devices  65 us (15%)
  between operations  13.6 us (3%)
  other arithmetic  11.7 us (3%)
  starting transfers between devices  8.94 us (2%)
  matrix products  5.45 us (1%)
    all_gather x1, blocking collectives, apply_channels(): lax.all_gather(kernel_rows, 'freq', axis=0, tiled=True)  69.7 us
    all_gather x1, waiting for transfers between devices, body(): lax.all_gather(time_kernel, 'tm', axis=0, tiled=True)  63.6 us
    all_gather x1, blocking collectives, apply_channels(): lax.all_gather(weight_rows, 'freq', axis=0, tiled=True)  61.3 us
    all_to_all x1, blocking collectives, body(): lax.all_to_all(sliced, 'tm', split_axis=2, concat_axis=0, tiled=True)  43.6 us
    all_to_all x1, blocking collectives, body(): lax.all_to_all(time_smooth.reshape(total_times, local_channels, 1, slab_w...  36.2 us
    all_to_all x1, blocking collectives, body(): lax.all_to_all(smoothed.reshape(1, sub_times, -1, components * columns),...  30.2 us
    unnamed x15, local copies, waits for them, and re-layouts  22.2 us
    all_to_all x2, local copies, waits for them, and re-layouts, body(): lax.all_to_all(time_smooth.reshape(total_times, local_channels, 1, slab_w...  19 us
  transfers between devices with their start and end apart: 3, of which 1 were waited for; matrix products, arithmetic and copies ran while one was open for 11% of the time, Pallas kernels for 0%

commit v1 on v0

v1 whole, which is shorter than its diff:
```python
import functools

import jax
import jax.numpy as jnp
from jax import lax
from jax.experimental import pallas as pl
from jax.experimental.pallas import tpu as pltpu
from jax.sharding import PartitionSpec as P

MESH = pl.DeviceIdType.MESH
BF16 = jnp.bfloat16
F32 = jnp.float32
SX, SY, SZ = 4, 8, 8
CHIPS = SX * SY * SZ
NT_DIMS = (((1,), (1,)), ((), ()))


def place():
    tm, freq = lax.axis_index("tm"), lax.axis_index("freq")
    return freq // 4, (freq % 4) * 2 + (tm // 2) % 2, tm // 4, tm % 2


def device(x, y, z, core):
    return (z * 4 + (y % 2) * 2 + core, x * 4 + y // 2)


def chip_slot(x, y, z):
    return (x * SY + y) * SZ + z


def exchange_kernel(
    jones, right, diagonal, cross, flags, t_weights, t_kernel, f_weights, f_kernel,
    out,
    jones32, right32, diagonal32, cross32, flags_wide, halves, wide32, packed,
    arrived, columns, time_mats, mixed, smooth, freq_own, freq_mats, outgoing,
    returned, parts,
    ready_y, ready_x, half_send, half_recv, tile_send, tile_recv, own_sem,
    mat_send, mat_recv, row_send, row_recv, pair_send, pair_recv,
    freq_send, freq_recv, fpair_send, fpair_recv, back_send, back_recv,
    last_send, last_recv,
):
    x, y, z, core = place()
    low, j = y % 2, x * 4 + y // 2
    sibling = device(x, y, z, 1 - core)

    def on_x(k):
        return device((x + k) % SX, y, z, core)

    def on_y(k):
        return device(x, (y + k) % SY, z, core)

    def on_z(k):
        return device(x, y, (z + k) % SZ, core)

    def signal(semaphore, target):
        pl.semaphore_signal(semaphore, inc=1, device_id=target, device_id_type=MESH)

    def remote(src, dst, send, recv, target):
        pltpu.make_async_remote_copy(
            src_ref=src, dst_ref=dst, send_sem=send, recv_sem=recv,
            device_id=target, device_id_type=MESH,
        ).start()

    def drain(ref, semaphore):
        pltpu.make_async_copy(ref, ref, semaphore).wait()

    barrier = pltpu.get_barrier_semaphore()
    signal(barrier, sibling)
    for k in range(1, SZ):
        signal(barrier, on_z(k))
    for k in range(1, SY):
        signal(barrier, on_y(k))
    for k in range(1, SX):
        signal(barrier, on_x(k))

    rows = 512

    def widen(step, _):
        at = pl.ds(pl.multiple_of(step * rows, rows), rows)
        jones32[at, :] = jones[at, :].astype(F32)
        right32[at, :] = right[at, :].astype(F32)
        return 0

    lax.fori_loop(0, 8, widen, 0)
    diagonal32[...] = diagonal[...].astype(F32)
    cross32[...] = cross[...].astype(F32)
    flagged = flags[...]
    flags_wide[...] = jnp.concatenate([flagged, flagged], axis=1)
    freq_own[0] = f_weights[...]
    freq_own[1] = f_kernel[...]

    def update(f, _):
        def part(ref, k, per):
            return ref[pl.ds(f * per + k, 32, stride=16 * per), :]

        keep = part(flags_wide, 0, 1) == 1
        upper, lower = part(diagonal32, 0, 2), part(diagonal32, 1, 2)
        real, imag = part(cross32, 0, 2), part(cross32, 1, 2)
        for offset in (0, 4):
            lead_r, lead_i, tail_r, tail_i = (part(right32, offset + k, 8) for k in range(4))
            entries = (
                lead_r * upper + tail_r * real + tail_i * imag,
                lead_i * upper + tail_i * real - tail_r * imag,
                lead_r * real - lead_i * imag + tail_r * lower,
                lead_r * imag + lead_i * real + tail_i * lower,
            )
            for k, entry in enumerate(entries):
                previous = part(jones32, offset + k, 8)
                value = jnp.where(keep, previous, 0.5 * previous + 0.5 * entry)
                halves[offset + k, f, core] = value.astype(BF16)
        return 0

    lax.fori_loop(0, 16, update, 0)

    pl.semaphore_wait(barrier, 1 + (SZ - 1) + (SY - 1) + (SX - 1))
    for k in range(1, SY):
        signal(ready_y, on_y(k))
    mine, other = pl.ds(core * 4, 4), pl.ds((1 - core) * 4, 4)
    remote(halves.at[other, :, core], halves.at[other, :, core], half_send, half_recv, sibling)
    pl.semaphore_wait(ready_y, SY - 1)
    for k in range(1, SX):
        signal(ready_x, on_x(k))

    quarter = pl.ds(pl.multiple_of(x * 256, 256), 256)
    block = z * 2 + low
    for m, source in enumerate((t_weights, t_kernel)):
        pltpu.make_async_copy(
            source.at[:, quarter], time_mats.at[m, block, core, :, quarter], own_sem.at[m]
        ).start()

        def send_rows(k, _, m=m, source=source):
            to_z, to_low = (z + k // 2) % SZ, (low + k) % 2
            remote(
                source.at[:, quarter], time_mats.at[m, block, core, :, quarter],
                row_send.at[m], row_recv.at[m],
                device(x, y - low + to_low, to_z, core),
            )
            return 0

        lax.fori_loop(1, 16, send_rows, 0)

    drain(halves.at[other, :, core], half_recv)

    def flip(f, _):
        for pair in range(2):
            stacked = jnp.concatenate(
                [
                    halves[core * 4 + pair * 2 + low, f].reshape(64, 128),
                    halves[core * 4 + pair * 2 + 1 - low, f].reshape(64, 128),
                ],
                axis=0,
            ).astype(F32)
            wide32[pl.ds(pair * 2048 + f, 128, stride=16), :] = stacked.T
        return 0

    lax.fori_loop(0, 16, flip, 0)

    def narrow(step, _):
        at = pl.ds(pl.multiple_of(step * rows, rows), rows)
        packed[at, :] = wide32[at, :].astype(BF16)
        return 0

    lax.fori_loop(0, 8, narrow, 0)

    pl.semaphore_wait(ready_x, SX - 1)
    own_freq = freq_mats.at[core, pl.ds(pl.multiple_of(j * 16, 16), 16)]
    pltpu.make_async_copy(freq_own.at[core], own_freq, own_sem.at[2]).start()

    def send_freq(k, _):
        to_x, to_y = (x + k // 4) % SX, (y + 2 * (k % 4)) % SY
        remote(freq_own.at[core], own_freq, freq_send, freq_recv, device(to_x, to_y, z, core))
        return 0

    lax.fori_loop(1, 16, send_freq, 0)

    def tile(index):
        return pl.ds(pl.multiple_of(index * 16, 16), 16)

    def chip_at(k):
        return (x + k // 64) % SX, (y + (k // 8) % 8) % SY, (z + k % 8) % SZ

    here = block * 16 + j
    me = chip_slot(x, y, z)
    own = pltpu.make_async_copy(packed.at[tile(me)], arrived.at[tile(here)], own_sem.at[3])
    own.start()

    def send_tile(k, _):
        cx, cy, cz = chip_at(k)
        remote(
            packed.at[tile(chip_slot(cx, cy, cz))], arrived.at[tile(here)],
            tile_send, tile_recv, device(cx, cy, cz, core),
        )
        return 0

    lax.fori_loop(1, CHIPS, send_tile, 0)

    for m in range(2):
        pltpu.make_async_copy(
            t_weights.at[:, quarter], time_mats.at[m, block, core, :, quarter], own_sem.at[m]
        ).wait()
        drain(time_mats.at[m, pl.ds(0, 15), core, :, pl.ds(0, 256)], row_recv.at[m])
        for k in range(1, SX):
            remote(
                time_mats.at[m, :, core, :, quarter], time_mats.at[m, :, core, :, quarter],
                mat_send.at[m], mat_recv.at[m], on_x(k),
            )
    pltpu.make_async_copy(freq_own.at[core], own_freq, own_sem.at[2]).wait()
    drain(freq_mats.at[core, pl.ds(0, 240)], freq_recv)
    remote(freq_mats.at[core], freq_mats.at[core], fpair_send, fpair_recv, sibling)
    for m in range(2):
        drain(time_mats.at[m, :, core, :, pl.ds(0, 768)], mat_recv.at[m])
        remote(
            time_mats.at[m, :, core], time_mats.at[m, :, core],
            pair_send.at[m], pair_recv.at[m], sibling,
        )
    drain(freq_mats.at[1 - core], fpair_recv)
    for m in range(2):
        drain(time_mats.at[m, :, 1 - core], pair_recv.at[m])

    own.wait()
    most = pl.ds(0, (CHIPS - 1) * 16)
    drain(arrived.at[most], tile_recv)

    left = lax.broadcasted_iota(jnp.int32, (256, 128), 1) < 64

    def merge(step, _):
        first = arrived[pl.ds(pl.multiple_of(step * 512, 512), 256), :].astype(F32)
        second = arrived[pl.ds(pl.multiple_of(step * 512 + 256, 256), 256), :].astype(F32)
        lanes = pl.ds(pl.multiple_of(step * 128, 128), 128)
        columns[pl.ds(0, 256), lanes] = jnp.where(left, first, second).astype(BF16)
        columns[pl.ds(256, 256), lanes] = pltpu.roll(
            jnp.where(left, second, first), 64, 1
        ).astype(BF16)
        return 0

    lax.fori_loop(0, SZ, merge, 0)

    def apply_time(m, source, target):
        def step(n, _):
            matrix = time_mats[m, pl.ds(n * 4, 4)].reshape(256, 1024)
            lanes = pl.ds(pl.multiple_of(n * 256, 256), 256)
            target[:, lanes] = lax.dot_general(
                source[...], matrix, NT_DIMS, preferred_element_type=F32
            ).astype(BF16)
            return 0

        lax.fori_loop(0, 4, step, 0)

    apply_time(0, columns, mixed)
    apply_time(1, mixed, smooth)

    def channels(n, _):
        lanes = pl.ds(pl.multiple_of(n * 128, 128), 128)
        results = []
        for c in range(2):
            step = jnp.dot(
                freq_mats[0], smooth[pl.ds(c * 256, 256), lanes], preferred_element_type=F32
            ).astype(BF16)
            results.append(jnp.dot(freq_mats[1], step, preferred_element_type=F32))
        turned = pltpu.roll(results[1], 64, 1)
        outgoing[pl.ds(pl.multiple_of(n * 512, 512), 256), :] = jnp.where(
            left, results[0], turned
        ).astype(BF16)
        outgoing[pl.ds(pl.multiple_of(n * 512 + 256, 256), 256), :] = jnp.where(
            left, turned, results[0]
        ).astype(BF16)
        return 0

    lax.fori_loop(0, SZ, channels, 0)

    back = pltpu.make_async_copy(outgoing.at[tile(here)], returned.at[tile(me)], own_sem.at[4])
    back.start()

    def send_back(k, _):
        cx, cy, cz = chip_at(k)
        there = (cz * 2 + cy % 2) * 16 + cx * 4 + cy // 2
        remote(
            outgoing.at[tile(there)], returned.at[tile(me)],
            back_send, back_recv, device(cx, cy, cz, core),
        )
        return 0

    lax.fori_loop(1, CHIPS, send_back, 0)
    back.wait()
    drain(returned.at[most], back_recv)

    def rewiden(step, _):
        at = pl.ds(pl.multiple_of(step * rows, rows), rows)
        right32[at, :] = returned[at, :].astype(F32)
        return 0

    lax.fori_loop(0, 8, rewiden, 0)

    def unflip(f, _):
        for pair in range(2):
            turned = right32[pl.ds(pair * 2048 + f, 128, stride=16), :].T.astype(BF16)
            parts[core * 4 + pair * 2 + low, f] = turned[:64].reshape(2, 32, 128)
            parts[core * 4 + pair * 2 + 1 - low, f] = turned[64:].reshape(2, 32, 128)
        return 0

    lax.fori_loop(0, 16, unflip, 0)

    keep_own = pltpu.make_async_copy(parts.at[mine, :, core], out.at[mine], own_sem.at[5])
    keep_own.start()
    remote(parts.at[mine, :, 1 - core], out.at[mine], last_send, last_recv, sibling)
    keep_own.wait()
    drain(out.at[other], last_recv)

    drain(out.at[mine], last_send)
    drain(halves.at[other, :, core], half_send)
    drain(packed.at[most], tile_send)
    drain(outgoing.at[most], back_send)
    drain(freq_mats.at[core, pl.ds(0, 240)], freq_send)
    drain(freq_mats.at[core], fpair_send)
    for m in range(2):
        drain(time_mats.at[m, pl.ds(0, 15), core, :, pl.ds(0, 256)], row_send.at[m])
        drain(time_mats.at[m, :, core, :, pl.ds(0, 768)], mat_send.at[m])
        drain(time_mats.at[m, :, core], pair_send.at[m])


def place_kernel(parts, out):
    def step(f, _):
        for k in range(8):
            out[pl.ds(f * 8 + k, 32, stride=128), :] = parts[k, f].astype(F32)
        return 0

    lax.fori_loop(0, 16, step, 0)


def body(
    jones_gains, right_terms, normal_diagonal, normal_cross, station_flags,
    time_weights, time_kernel, channel_weights, channel_kernel,
):
    vmem = pl.BlockSpec(memory_space=pltpu.VMEM)
    dma = pltpu.SemaphoreType.DMA
    parts = pl.pallas_call(
        exchange_kernel,
        out_shape=jax.ShapeDtypeStruct((8, 16, 32, 128), BF16),
        in_specs=[vmem] * 9,
        out_specs=vmem,
        scratch_shapes=[
            pltpu.VMEM((4096, 128), F32),
            pltpu.VMEM((4096, 128), F32),
            pltpu.VMEM((1024, 128), F32),
            pltpu.VMEM((1024, 128), F32),
            pltpu.VMEM((512, 128), jnp.int32),
            pltpu.VMEM((8, 16, 2, 32, 128), BF16),
            pltpu.VMEM((4096, 128), F32),
            pltpu.VMEM((4096, 128), BF16),
            pltpu.VMEM((4096, 128), BF16),
            pltpu.VMEM((512, 1024), BF16),
            pltpu.VMEM((2, 16, 2, 32, 1024), BF16),
            pltpu.VMEM((512, 1024), BF16),
            pltpu.VMEM((512, 1024), BF16),
            pltpu.VMEM((2, 16, 256), BF16),
            pltpu.VMEM((2, 256, 256), BF16),
            pltpu.VMEM((4096, 128), BF16),
            pltpu.VMEM((4096, 128), BF16),
            pltpu.VMEM((8, 16, 2, 32, 128), BF16),
            pltpu.SemaphoreType.REGULAR,
            pltpu.SemaphoreType.REGULAR,
            dma, dma, dma, dma,
            dma((6,)),
            dma((2,)), dma((2,)), dma((2,)), dma((2,)), dma((2,)), dma((2,)),
            dma, dma, dma, dma, dma, dma, dma, dma,
        ],
        compiler_params=pltpu.CompilerParams(
            collective_id=0, has_side_effects=True, vmem_limit_bytes=48 * 1024 * 1024
        ),
    )(
        jones_gains.reshape(4096, 128),
        right_terms.reshape(4096, 128),
        normal_diagonal.reshape(1024, 128),
        normal_cross.reshape(1024, 128),
        station_flags.reshape(512, 64),
        time_weights, time_kernel, channel_weights, channel_kernel,
    )
    placed = pl.pallas_call(
        place_kernel,
        out_shape=jax.ShapeDtypeStruct((4096, 128), F32),
        in_specs=[vmem],
        out_specs=vmem,
        compiler_params=pltpu.CompilerParams(vmem_limit_bytes=16 * 1024 * 1024),
    )(parts)
    return placed.reshape(32, 16, 8, 128)


def solution(mesh):
    cells = P("tm", "freq", None, None)
    in_specs = (
        cells, cells, cells, cells, P("tm", "freq", None),
        P("tm", None), P("tm", None), P("freq", None), P("freq", None),
    )
    return jax.shard_map(body, mesh=mesh, in_specs=in_specs, out_specs=cells, check_vma=False)
```

time: 430 us -> 124 us (0.29)
  the two profiles are of different devices: /device:TPU:8 before, /device:TPU:1 now
where the time goes in v1:
time: 124 us
  Pallas kernels  115 us (93%)
  local copies, waits for them, and re-layouts  8.37 us (7%)
    pallas_call x1, Pallas kernels, body(): pl.pallas_call(exchange_kernel, out_shape=jax.ShapeDtypeStruct((8, 16, 32...  112 us
    unnamed x18, local copies, waits for them, and re-layouts  8.37 us
    pallas_call x1, Pallas kernels, body(): pl.pallas_call(place_kernel, out_shape=jax.ShapeDtypeStruct((4096, 128),...  3.29 us

profile of v1, /device:TPU:1, one launch (start us, length us, event | category | flops | bytes accessed | tf_op | source)
XLA Modules:
  0.0 123.8 jit_solution(16459700017727023058)
XLA Ops:
  0.0 0.0 copy-start
  0.0 1.2 copy-done
  1.2 0.0 copy-start.1
  1.2 1.2 copy-done.1
  2.5 0.0 copy-start.2
  2.5 0.9 copy-done.2
  3.4 0.0 copy-start.3
  3.4 0.9 copy-done.3
  4.4 0.0 copy-start.4
  4.4 0.9 copy-done.4
  5.3 0.0 copy-start.5
  5.3 0.8 copy-done.5
  6.1 0.0 copy-start.6
  6.1 0.8 copy-done.6
  7.0 0.0 copy-start.7
  7.0 0.7 copy-done.7
  7.7 0.0 copy-start.8
  7.7 0.7 copy-done.8
  8.4 112.1 %shard_map.91.parts = bf16[8,16,32,128]{3,2,1,0:T(8,128)(2,1)S(1)} custom-call(bf16[4096,128]{1,0:T(8,128)(2,1)S(1)} %bitcast.6, bf16[4096,128]{1,0:T(8,128)(2,1)S(1)} %bitcast.7, bf16[1024,128]{1,0:T(8,128)(2,1)S(1)} %bitcast.8, bf16[1024,128]{1,0:T(8,128)(2,1)S(1)} %bitcast.9, s32[512,64]{1,0:T(8,128)S(1)} %bitcast.10, bf16[32,1024]{1,0:T(8,128)(2,1)S(1)} %copy-done.5, ...), custom_call_target="tpu_custom_call" | custom-call | tf_op jit(solution)/shard_map/pallas_call | solution.py:336
  120.5 3.3 %shard_map.92 = f32[4096,128]{1,0:T(8,128)} custom-call(bf16[8,16,32,128]{3,2,1,0:T(8,128)(2,1)S(1)} %shard_map.91.parts), custom_call_target="tpu_custom_call" | custom-call | tf_op jit(solution)/shard_map/pallas_call | solution.py:378
Async XLA Ops:
  0.0 1.2 copy-start
  1.2 1.2 copy-start.1
  2.5 0.9 copy-start.2
  3.4 0.9 copy-start.3
  4.4 0.9 copy-start.4
  5.3 0.8 copy-start.5
  6.1 0.8 copy-start.6
  7.0 0.7 copy-start.7
  7.7 0.7 copy-start.8

commit v2 on v1

v2 whole, which is shorter than its diff:
```python
import functools

import jax
import jax.numpy as jnp
from jax import lax
from jax.experimental import pallas as pl
from jax.experimental.pallas import tpu as pltpu
from jax.sharding import PartitionSpec as P

MESH = pl.DeviceIdType.MESH
BF16 = jnp.bfloat16
F32 = jnp.float32
SX, SY, SZ = 4, 8, 8
CHIPS = SX * SY * SZ
MATS = True
CELL, PAIR, FLAG, TILE = 136, 40, 24, 17
NT_DIMS = (((1,), (1,)), ((), ()))


def place():
    tm, freq = lax.axis_index("tm"), lax.axis_index("freq")
    return freq // 4, (freq % 4) * 2 + (tm // 2) % 2, tm // 4, tm % 2


def device(x, y, z, core):
    return (z * 4 + (y % 2) * 2 + core, x * 4 + y // 2)


def chip_slot(x, y, z):
    return (((x % 2) * 2 + x // 2) * SY + y) * SZ + z


def exchange_kernel(
    jones_in, right_in, diagonal_in, cross_in, flags_in, t_weights_in, t_kernel_in,
    f_weights_in, f_kernel_in,
    out,
    jones, right, diagonal, cross, flags, rows_own, freq_own,
    jones32, right32, diagonal32, cross32, flags_wide, halves, wide32, packed,
    arrived, columns, time_mats, mixed, smooth, freq_mats, outgoing,
    returned, parts,
    ready_y, ready_x, load_sem, half_send, half_recv, tile_send, tile_recv, own_sem,
    row_send, row_recv, side_send, side_recv, far_send, far_recv, pair_send, pair_recv,
    freq_send, freq_recv, fpair_send, fpair_recv, back_send, back_recv,
    last_send, last_recv,
):
    x, y, z, core = place()
    low, j = y % 2, x * 4 + y // 2
    block = z * 2 + low
    here = block * 16 + j
    me = chip_slot(x, y, z)
    sibling = device(x, y, z, 1 - core)
    mine, other = pl.ds(core * 4, 4), pl.ds((1 - core) * 4, 4)

    def on_x(k):
        return device((x + k) % SX, y, z, core)

    def on_y(k):
        return device(x, (y + k) % SY, z, core)

    def in_time(k):
        return device(x, y - low + (low + k) % 2, (z + k // 2) % SZ, core)

    def signal(semaphore, target):
        pl.semaphore_signal(semaphore, inc=1, device_id=target, device_id_type=MESH)

    def remote(src, dst, send, recv, target):
        pltpu.make_async_remote_copy(
            src_ref=src, dst_ref=dst, send_sem=send, recv_sem=recv,
            device_id=target, device_id_type=MESH,
        ).start()

    def drain(ref, semaphore):
        pltpu.make_async_copy(ref, ref, semaphore).wait()

    def tile(index):
        return pl.ds(pl.multiple_of(index * 16, 16), 16)

    barrier = pltpu.get_barrier_semaphore()
    signal(barrier, sibling)
    for k in range(1, 16):
        signal(barrier, in_time(k))
    for k in range(1, SY):
        @pl.when((y + k) % SY // 2 != y // 2)
        def _(k=k):
            signal(barrier, on_y(k))
    for k in range(1, SX):
        signal(barrier, on_x(k))

    loads = [
        pltpu.make_async_copy(src, dst, load_sem.at[n])
        for n, (src, dst) in enumerate(
            (
                (t_weights_in, rows_own.at[0]), (t_kernel_in, rows_own.at[1]),
                (f_weights_in, freq_own.at[0]), (f_kernel_in, freq_own.at[1]),
                (right_in, right), (jones_in, jones), (diagonal_in, diagonal),
                (cross_in, cross), (flags_in, flags),
            )
        )
    ]
    for load in loads:
        load.start()
    for load in loads:
        load.wait()

    def spread(t, _):
        def move(src, dst, per, pitch):
            value = src[pl.ds(pl.multiple_of(t * per, per), per), :]
            dst[pl.ds(pl.multiple_of(t * pitch, 8), per), :] = value.astype(dst.dtype)

        move(jones, jones32, 128, CELL)
        move(right, right32, 128, CELL)
        move(diagonal, diagonal32, 32, PAIR)
        move(cross, cross32, 32, PAIR)
        flagged = flags[pl.ds(pl.multiple_of(t * 16, 16), 16), :]
        flags_wide[pl.ds(pl.multiple_of(t * FLAG, 8), 16), :] = jnp.concatenate(
            [flagged, flagged], axis=1
        )
        return 0

    lax.fori_loop(0, 32, spread, 0)

    def update(f, _):
        def part(ref, k, per, pitch):
            return ref[pl.ds(f * per + k, 32, stride=pitch), :]

        keep = part(flags_wide, 0, 1, FLAG) == 1
        upper, lower = part(diagonal32, 0, 2, PAIR), part(diagonal32, 1, 2, PAIR)
        real, imag = part(cross32, 0, 2, PAIR), part(cross32, 1, 2, PAIR)
        for offset in (0, 4):
            lead_r, lead_i, tail_r, tail_i = (
                part(right32, offset + k, 8, CELL) for k in range(4)
            )
            entries = (
                lead_r * upper + tail_r * real + tail_i * imag,
                lead_i * upper + tail_i * real - tail_r * imag,
                lead_r * real - lead_i * imag + tail_r * lower,
                lead_r * imag + lead_i * real + tail_i * lower,
            )
            for k, entry in enumerate(entries):
                previous = part(jones32, offset + k, 8, CELL)
                value = jnp.where(keep, previous, 0.5 * previous + 0.5 * entry)
                halves[offset + k, f, core] = value.astype(BF16)
        return 0

    def update_some(c):
        lax.fori_loop(c * 4, c * 4 + 4, update, 0)

    def send_half(c):
        some = halves.at[other, pl.ds(c * 8, 8), core]
        remote(some, some, half_send.at[c], half_recv.at[c], sibling)

    update_some(0)
    pl.semaphore_wait(barrier, 1 + 15 + (SY - 2) + (SX - 1))
    for k in range(1, SY):
        signal(ready_y, on_y(k))

    quarter = pl.ds(pl.multiple_of(x * 256, 256), 256)

    def own_rows(m):
        return pltpu.make_async_copy(
            rows_own.at[m, :, quarter], time_mats.at[m, block, core, :, quarter], own_sem.at[m]
        )

    for m in range(2 if MATS else 0):
        own_rows(m).start()

        def send_rows(k, _, m=m):
            remote(
                rows_own.at[m, :, quarter], time_mats.at[m, block, core, :, quarter],
                row_send.at[m], row_recv.at[m], in_time(k),
            )
            return 0

        lax.fori_loop(1, 16, send_rows, 0)

    own_channels = freq_mats.at[core, x, y // 2]
    freq_mats[core, x, y // 2] = freq_own[core]
    for k in range(1, SX):
        remote(own_channels, own_channels, freq_send.at[0], freq_recv.at[0], on_x(k))

    update_some(1)
    send_half(0)
    drain(freq_mats.at[core, pl.ds(0, 3), 0], freq_recv.at[0])
    column_channels = freq_mats.at[core, :, y // 2]
    for k in range(2, SY, 2):
        remote(column_channels, column_channels, freq_send.at[1], freq_recv.at[1], on_y(k))
    pl.semaphore_wait(ready_y, SY - 1)
    for k in range(1, SX):
        signal(ready_x, on_x(k))
    update_some(2)
    update_some(3)
    send_half(1)

    def send_sides(m):
        own_rows(m).wait()
        drain(time_mats.at[m, pl.ds(0, 15), core, :, pl.ds(0, 256)], row_recv.at[m])
        ref = time_mats.at[m, :, core, :, quarter]
        remote(ref, ref, side_send.at[m, 0], side_recv.at[m, 0], on_x(1))
        remote(ref, ref, side_send.at[m, 1], side_recv.at[m, 1], on_x(SX - 1))

    def quarter_of(k):
        return pl.ds(pl.multiple_of((x + k) % SX * 256, 256), 256)

    def forward_sides(m):
        ref = time_mats.at[m, pl.ds(0, 8), core, :, quarter_of(SX - 1)]
        drain(time_mats.at[m, :, core, :, quarter_of(SX - 1)], side_recv.at[m, 0])
        remote(ref, ref, far_send.at[m, 0], far_recv.at[m, 0], on_x(1))
        ref = time_mats.at[m, pl.ds(8, 8), core, :, quarter_of(1)]
        drain(time_mats.at[m, :, core, :, quarter_of(1)], side_recv.at[m, 1])
        remote(ref, ref, far_send.at[m, 1], far_recv.at[m, 1], on_x(SX - 1))

    def send_pair(m):
        for side in range(2):
            drain(time_mats.at[m, pl.ds(0, 8), core, :, quarter_of(2)], far_recv.at[m, side])
        ref = time_mats.at[m, :, core]
        remote(ref, ref, pair_send.at[m], pair_recv.at[m], sibling)

    def flip_pair(pair):
        def flip(f, _):
            stacked = jnp.concatenate(
                [
                    halves[core * 4 + pair * 2 + low, f].reshape(64, 128),
                    halves[core * 4 + pair * 2 + 1 - low, f].reshape(64, 128),
                ],
                axis=0,
            )
            wide32[pl.ds(pair * 128 * TILE + f, 128, stride=TILE), :] = stacked.T.astype(F32)
            return 0

        return flip

    def narrow_pair(pair):
        def narrow(step, _):
            for k in range(16):
                index = pair * 128 + step * 16 + k
                packed[tile(index), :] = wide32[pl.ds(index * TILE, 16), :].astype(BF16)
            return 0

        lax.fori_loop(0, 8, narrow, 0)

    def send_tiles(part):
        pair = odd if part < 4 else 1 - odd

        def send_tile(k, _):
            cx = (x // 2 + k // 64) % 2 * 2 + pair
            turn = k // 8 % 8
            cy, cz = (y + turn % 4 * 2 + turn // 4) % SY, (z + k) % SZ
            remote(
                packed.at[tile(chip_slot(cx, cy, cz))], arrived.at[tile(here)],
                tile_send.at[part], tile_recv, device(cx, cy, cz, core),
            )
            return 0

        start = part % 4 * 32
        lax.fori_loop(start + (part == 0), start + 32, send_tile, 0)

    def tiles_sent(part):
        drain(packed.at[pl.ds(0, 496 if part == 0 else 512)], tile_send.at[part])

    odd = x % 2
    for c in range(2):
        drain(halves.at[other, pl.ds(c * 8, 8), core], half_recv.at[c])
        lax.fori_loop(c * 8, c * 8 + 8, flip_pair(odd), 0)
    narrow_pair(odd)
    pl.semaphore_wait(ready_x, SX - 1)
    drain(freq_mats.at[core, :, pl.ds(0, 3)], freq_recv.at[1])
    remote(freq_mats.at[core], freq_mats.at[core], fpair_send, fpair_recv, sibling)
    own = pltpu.make_async_copy(packed.at[tile(me)], arrived.at[tile(here)], own_sem.at[3])
    own.start()
    if MATS:
        send_sides(0)
    send_tiles(0)
    send_tiles(1)
    lax.fori_loop(0, 16, flip_pair(1 - odd), 0)
    narrow_pair(1 - odd)
    if MATS:
        send_sides(1)
    tiles_sent(0)
    send_tiles(2)
    tiles_sent(1)
    send_tiles(3)
    tiles_sent(2)
    send_tiles(4)
    if MATS:
        forward_sides(0)
    tiles_sent(3)
    send_tiles(5)
    if MATS:
        forward_sides(1)
    tiles_sent(4)
    send_tiles(6)
    if MATS:
        send_pair(0)
    tiles_sent(5)
    send_tiles(7)
    if MATS:
        send_pair(1)
    drain(freq_mats.at[1 - core], fpair_recv)

    own.wait()
    most = pl.ds(0, (CHIPS - 1) * 16)
    drain(arrived.at[most], tile_recv)

    left = lax.broadcasted_iota(jnp.int32, (256, 128), 1) < 64

    def merge(step, _):
        first = arrived[pl.ds(pl.multiple_of(step * 512, 512), 256), :].astype(F32)
        second = arrived[pl.ds(pl.multiple_of(step * 512 + 256, 256), 256), :].astype(F32)
        lanes = pl.ds(pl.multiple_of(step * 128, 128), 128)
        columns[pl.ds(0, 256), lanes] = jnp.where(left, first, second).astype(BF16)
        columns[pl.ds(256, 256), lanes] = pltpu.roll(
            jnp.where(left, second, first), 64, 1
        ).astype(BF16)
        return 0

    lax.fori_loop(0, SZ, merge, 0)

    def times(m, source, n):
        matrix = time_mats[m, pl.ds(n * 4, 4)].reshape(256, 1024)
        return lax.dot_general(source[...], matrix, NT_DIMS, preferred_element_type=F32)

    if MATS:
        drain(time_mats.at[0, :, 1 - core], pair_recv.at[0])

    def first_times(n, _):
        mixed[:, pl.ds(pl.multiple_of(n * 256, 256), 256)] = times(0, columns, n).astype(BF16)
        return 0

    lax.fori_loop(0, 4, first_times, 0)

    first_channels, second_channels = (freq_mats[m].reshape(256, 256) for m in range(2))

    def channels(n, _):
        lanes = pl.ds(pl.multiple_of(n % 2 * 512, 512), 512)
        at = pl.ds(pl.multiple_of(n // 2 * 256, 256), 256)
        step = jnp.dot(first_channels, mixed[at, lanes], preferred_element_type=F32).astype(BF16)
        smooth[at, lanes] = jnp.dot(
            second_channels, step, preferred_element_type=F32
        ).astype(BF16)
        return 0

    lax.fori_loop(0, 4, channels, 0)

    back = pltpu.make_async_copy(outgoing.at[tile(here)], returned.at[tile(me)], own_sem.at[4])
    if MATS:
        drain(time_mats.at[1, :, 1 - core], pair_recv.at[1])

    def second_times(step, _):
        ahead = (3 - step) % 4
        pair = ((z + ahead) % SZ, (z + jnp.where(ahead == 0, 4, SZ - ahead)) % SZ)
        matrix = jnp.concatenate(
            [time_mats[1, pl.ds(cz * 2, 2)].reshape(128, 1024) for cz in pair], axis=0
        )
        result = lax.dot_general(smooth[...], matrix, NT_DIMS, preferred_element_type=F32)
        for half, cz in enumerate(pair):
            kept = result[:256, half * 128 : half * 128 + 128]
            turned = pltpu.roll(result[256:, half * 128 : half * 128 + 128], 64, 1)
            outgoing[pl.ds(pl.multiple_of(cz * 512, 512), 256), :] = jnp.where(
                left, kept, turned
            ).astype(BF16)
            outgoing[pl.ds(pl.multiple_of(cz * 512 + 256, 256), 256), :] = jnp.where(
                left, turned, kept
            ).astype(BF16)

        def send_back(k, _):
            cx, cy = (x + k // 16) % SX, (y + k // 2) % SY
            cz = jnp.where(k % 2 == 0, pair[0], pair[1])
            there = (cz * 2 + cy % 2) * 16 + cx * 4 + cy // 2

            @pl.when(there != here)
            def _():
                remote(
                    outgoing.at[tile(there)], returned.at[tile(me)],
                    back_send, back_recv, device(cx, cy, cz, core),
                )

            return 0

        lax.fori_loop(0, 64, send_back, 0)
        return 0

    lax.fori_loop(0, 4, second_times, 0)
    back.start()
    back.wait()
    drain(returned.at[most], back_recv)

    def rewiden(step, _):
        for k in range(16):
            index = step * 16 + k
            wide32[pl.ds(index * TILE, 16), :] = returned[tile(index), :].astype(F32)
        return 0

    lax.fori_loop(0, 16, rewiden, 0)

    def unflip(f, _):
        for pair in range(2):
            turned = wide32[pl.ds(pair * 128 * TILE + f, 128, stride=TILE), :].astype(BF16).T
            parts[core * 4 + pair * 2 + low, f] = turned[:64].reshape(2, 32, 128)
            parts[core * 4 + pair * 2 + 1 - low, f] = turned[64:].reshape(2, 32, 128)
        return 0

    def keep_own(c):
        some = pl.ds(c * 4, 4)
        return pltpu.make_async_copy(
            parts.at[mine, some, core], out.at[mine, some], own_sem.at[5 + c]
        )

    for c in range(4):
        lax.fori_loop(c * 4, c * 4 + 4, unflip, 0)
        keep_own(c).start()
        some = pl.ds(c * 4, 4)
        remote(
            parts.at[mine, some, 1 - core], out.at[mine, some],
            last_send.at[c], last_recv.at[c], sibling,
        )
    for c in range(4):
        keep_own(c).wait()
        drain(out.at[other, pl.ds(c * 4, 4)], last_recv.at[c])

    for c in range(4):
        drain(out.at[mine, pl.ds(c * 4, 4)], last_send.at[c])
    for c in range(2):
        drain(halves.at[other, pl.ds(c * 8, 8), core], half_send.at[c])
    tiles_sent(6)
    tiles_sent(7)
    drain(outgoing.at[most], back_send)
    drain(freq_mats.at[core, pl.ds(0, 3), 0], freq_send.at[0])
    drain(freq_mats.at[core, :, pl.ds(0, 3)], freq_send.at[1])
    drain(freq_mats.at[core], fpair_send)
    for m in range(2 if MATS else 0):
        drain(time_mats.at[m, pl.ds(0, 15), core, :, pl.ds(0, 256)], row_send.at[m])
        for side in range(2):
            drain(time_mats.at[m, :, core, :, pl.ds(0, 256)], side_send.at[m, side])
            drain(time_mats.at[m, pl.ds(0, 8), core, :, pl.ds(0, 256)], far_send.at[m, side])
        drain(time_mats.at[m, :, core], pair_send.at[m])


def place_kernel(parts, out):
    def step(f, _):
        for k in range(8):
            out[pl.ds(f * 8 + k, 16, stride=128), :] = parts[k, f].astype(F32)
        return 0

    lax.fori_loop(0, 16, step, 0)


def body(
    jones_gains, right_terms, normal_diagonal, normal_cross, station_flags,
    time_weights, time_kernel, channel_weights, channel_kernel,
):
    dma = pltpu.SemaphoreType.DMA
    scratch = [
        ((4096, 128), BF16), ((4096, 128), BF16), ((1024, 128), BF16), ((1024, 128), BF16),
        ((512, 64), jnp.int32), ((2, 32, 1024), BF16), ((2, 16, 256), BF16),
        ((32 * CELL, 128), F32), ((32 * CELL, 128), F32),
        ((32 * PAIR, 128), F32), ((32 * PAIR, 128), F32),
        ((32 * FLAG, 128), jnp.int32), ((8, 16, 2, 32, 128), BF16), ((CHIPS * TILE, 128), F32),
        ((4096, 128), BF16), ((4096, 128), BF16), ((512, 1024), BF16),
        ((2, 16, 2, 32, 1024), BF16), ((512, 1024), BF16), ((512, 1024), BF16),
        ((2, 4, 4, 16, 256), BF16), ((4096, 128), BF16), ((4096, 128), BF16),
        ((8, 16, 2, 32, 128), BF16),
    ]
    parts = pl.pallas_call(
        exchange_kernel,
        out_shape=jax.ShapeDtypeStruct((8, 16, 32, 128), BF16),
        in_specs=[pl.BlockSpec(memory_space=pltpu.HBM)] * 9,
        out_specs=pl.BlockSpec(memory_space=pltpu.VMEM),
        scratch_shapes=[
            *(pltpu.VMEM(shape, dtype) for shape, dtype in scratch),
            pltpu.SemaphoreType.REGULAR,
            pltpu.SemaphoreType.REGULAR,
            dma((9,)), dma((2,)), dma((2,)), dma((8,)), dma, dma((9,)),
            dma((2,)), dma((2,)), dma((2, 2)), dma((2, 2)), dma((2, 2)), dma((2, 2)),
            dma((2,)), dma((2,)),
            dma((2,)), dma((2,)), dma, dma, dma, dma, dma((4,)), dma((4,)),
        ],
        compiler_params=pltpu.CompilerParams(
            collective_id=0, has_side_effects=True, vmem_limit_bytes=56 * 1024 * 1024
        ),
    )(
        jones_gains.reshape(4096, 128),
        right_terms.reshape(4096, 128),
        normal_diagonal.reshape(1024, 128),
        normal_cross.reshape(1024, 128),
        station_flags.reshape(512, 64),
        time_weights, time_kernel, channel_weights, channel_kernel,
    )
    placed = pl.pallas_call(
        place_kernel,
        grid=(2,),
        out_shape=jax.ShapeDtypeStruct((4096, 128), F32),
        in_specs=[pl.BlockSpec((8, 16, 16, 128), lambda n: (0, 0, n, 0))],
        out_specs=pl.BlockSpec((2048, 128), lambda n: (n, 0)),
        compiler_params=pltpu.CompilerParams(vmem_limit_bytes=16 * 1024 * 1024),
    )(parts)
    return placed.reshape(32, 16, 8, 128)


def solution(mesh):
    cells = P("tm", "freq", None, None)
    in_specs = (
        cells, cells, cells, cells, P("tm", "freq", None),
        P("tm", None), P("tm", None), P("freq", None), P("freq", None),
    )
    return jax.shard_map(body, mesh=mesh, in_specs=in_specs, out_specs=cells, check_vma=False)
```

time: 124 us -> 102 us (0.82)
  Pallas kernels: 115 us -> 101 us
  local copies, waits for them, and re-layouts: 8.37 us -> 1.22 us
    pallas_call x1, Pallas kernels: 112 us -> 97.9 us  [body(): pl.pallas_call(exchange_kernel, out_shape=jax.ShapeDtypeStruct((8, 16, 32...]
    unnamed x18 -> x2, local copies, waits for them, and re-layouts: 8.37 us -> 1.22 us
where the time goes in v2:
time: 102 us
  Pallas kernels  101 us (99%)
  local copies, waits for them, and re-layouts  1.22 us (1%)
    pallas_call x1, Pallas kernels, body(): pl.pallas_call(exchange_kernel, out_shape=jax.ShapeDtypeStruct((8, 16, 32...  97.9 us
    pallas_call x1, Pallas kernels, body(): pl.pallas_call(place_kernel, grid=(2,), out_shape=jax.ShapeDtypeStruct((4...  2.89 us

profile of v2, /device:TPU:1, one launch (start us, length us, event | category | flops | bytes accessed | tf_op | source)
XLA Modules:
  0.0 102.1 jit_solution(12103924666825110224)
XLA Ops:
  0.0 97.9 %shard_map.91.parts = bf16[8,16,32,128]{3,2,1,0:T(8,128)(2,1)} custom-call(bf16[4096,128]{1,0:T(8,128)(2,1)} %bitcast.6, bf16[4096,128]{1,0:T(8,128)(2,1)} %bitcast.7, bf16[1024,128]{1,0:T(8,128)(2,1)} %bitcast.8, bf16[1024,128]{1,0:T(8,128)(2,1)} %bitcast.9, s32[512,64]{1,0:T(8,128)} %bitcast.10, bf16[32,1024]{1,0:T(8,128)(2,1)} %t_weights_in.1, ...), custom_call_target="tpu_custom_call" | custom-call | tf_op jit(solution)/shard_map/pallas_call | solution.py:463
  97.9 0.0 copy-start
  97.9 1.2 %copy-done = bf16[8,16,32,128]{3,2,1,0:T(8,128)(2,1)S(1)} copy-done((bf16[8,16,32,128]{3,2,1,0:T(8,128)(2,1)S(1)}, bf16[8,16,32,128]{3,2,1,0:T(8,128)(2,1)}, u32[]{:S(2)}) %copy-start) | copy-done | bytes 1048600
  99.2 2.9 %shard_map.92 = f32[4096,128]{1,0:T(8,128)} custom-call(bf16[8,16,32,128]{3,2,1,0:T(8,128)(2,1)S(1)} %copy-done), custom_call_target="tpu_custom_call" | custom-call | tf_op jit(solution)/shard_map/pallas_call | solution.py:488
Async XLA Ops:
  97.9 1.2 %copy-start = (bf16[8,16,32,128]{3,2,1,0:T(8,128)(2,1)S(1)}, bf16[8,16,32,128]{3,2,1,0:T(8,128)(2,1)}, u32[]{:S(2)}) copy-start(bf16[8,16,32,128]{3,2,1,0:T(8,128)(2,1)} %shard_map.91.parts) | copy-start | bytes 3145732

commit v3 on v2

--- a/solution.py
+++ b/solution.py
@@ -12,7 +12,6 @@
 F32 = jnp.float32
 SX, SY, SZ = 4, 8, 8
 CHIPS = SX * SY * SZ
-MATS = True
 CELL, PAIR, FLAG, TILE = 136, 40, 24, 17
 NT_DIMS = (((1,), (1,)), ((), ()))
 
@@ -161,7 +160,7 @@
             rows_own.at[m, :, quarter], time_mats.at[m, block, core, :, quarter], own_sem.at[m]
         )
 
-    for m in range(2 if MATS else 0):
+    for m in range(2):
         own_rows(m).start()
 
         def send_rows(k, _, m=m):
@@ -267,34 +266,28 @@
     remote(freq_mats.at[core], freq_mats.at[core], fpair_send, fpair_recv, sibling)
     own = pltpu.make_async_copy(packed.at[tile(me)], arrived.at[tile(here)], own_sem.at[3])
     own.start()
-    if MATS:
-        send_sides(0)
+    send_sides(0)
     send_tiles(0)
     send_tiles(1)
     lax.fori_loop(0, 16, flip_pair(1 - odd), 0)
     narrow_pair(1 - odd)
-    if MATS:
-        send_sides(1)
+    send_sides(1)
     tiles_sent(0)
     send_tiles(2)
     tiles_sent(1)
     send_tiles(3)
     tiles_sent(2)
     send_tiles(4)
-    if MATS:
-        forward_sides(0)
+    forward_sides(0)
     tiles_sent(3)
     send_tiles(5)
-    if MATS:
-        forward_sides(1)
+    forward_sides(1)
     tiles_sent(4)
     send_tiles(6)
-    if MATS:
-        send_pair(0)
+    send_pair(0)
     tiles_sent(5)
     send_tiles(7)
-    if MATS:
-        send_pair(1)
+    send_pair(1)
     drain(freq_mats.at[1 - core], fpair_recv)
 
     own.wait()
@@ -319,31 +312,22 @@
         matrix = time_mats[m, pl.ds(n * 4, 4)].reshape(256, 1024)
         return lax.dot_general(source[...], matrix, NT_DIMS, preferred_element_type=F32)
 
-    if MATS:
-        drain(time_mats.at[0, :, 1 - core], pair_recv.at[0])
-
-    def first_times(n, _):
-        mixed[:, pl.ds(pl.multiple_of(n * 256, 256), 256)] = times(0, columns, n).astype(BF16)
-        return 0
-
-    lax.fori_loop(0, 4, first_times, 0)
+    drain(time_mats.at[0, :, 1 - core], pair_recv.at[0])
+
+    for n in range(4):
+        mixed[:, n * 256 : n * 256 + 256] = times(0, columns, n).astype(BF16)
 
     first_channels, second_channels = (freq_mats[m].reshape(256, 256) for m in range(2))
 
-    def channels(n, _):
-        lanes = pl.ds(pl.multiple_of(n % 2 * 512, 512), 512)
-        at = pl.ds(pl.multiple_of(n // 2 * 256, 256), 256)
-        step = jnp.dot(first_channels, mixed[at, lanes], preferred_element_type=F32).astype(BF16)
-        smooth[at, lanes] = jnp.dot(
+    for c in range(2):
+        at = pl.ds(c * 256, 256)
+        step = jnp.dot(first_channels, mixed[at, :], preferred_element_type=F32).astype(BF16)
+        smooth[at, :] = jnp.dot(
             second_channels, step, preferred_element_type=F32
         ).astype(BF16)
-        return 0
-
-    lax.fori_loop(0, 4, channels, 0)
 
     back = pltpu.make_async_copy(outgoing.at[tile(here)], returned.at[tile(me)], own_sem.at[4])
-    if MATS:
-        drain(time_mats.at[1, :, 1 - core], pair_recv.at[1])
+    drain(time_mats.at[1, :, 1 - core], pair_recv.at[1])
 
     def second_times(step, _):
         ahead = (3 - step) % 4
@@ -427,7 +411,7 @@
     drain(freq_mats.at[core, pl.ds(0, 3), 0], freq_send.at[0])
     drain(freq_mats.at[core, :, pl.ds(0, 3)], freq_send.at[1])
     drain(freq_mats.at[core], fpair_send)
-    for m in range(2 if MATS else 0):
+    for m in range(2):
         drain(time_mats.at[m, pl.ds(0, 15), core, :, pl.ds(0, 256)], row_send.at[m])
         for side in range(2):
             drain(time_mats.at[m, :, core, :, pl.ds(0, 256)], side_send.at[m, side])
@@ -435,13 +419,27 @@
         drain(time_mats.at[m, :, core], pair_send.at[m])
 
 
-def place_kernel(parts, out):
-    def step(f, _):
-        for k in range(8):
-            out[pl.ds(f * 8 + k, 16, stride=128), :] = parts[k, f].astype(F32)
-        return 0
-
-    lax.fori_loop(0, 16, step, 0)
+def place_kernel(parts, out, spread, store_sem):
+    for h in range(2):
+        def step(f, _, h=h):
+            for k in range(8):
+                spread[pl.ds(h * 16 * CELL + f * 8 + k, 16, stride=CELL), :] = parts[
+                    k, f, pl.ds(h * 16, 16)
+                ].astype(F32)
+            return 0
+
+        lax.fori_loop(0, 16, step, 0)
+
+        def store(t, _):
+            pltpu.make_async_copy(
+                spread.at[pl.ds(pl.multiple_of(t * CELL, 8), 128)],
+                out.at[pl.ds(pl.multiple_of(t * 128, 128), 128)],
+                store_sem,
+            ).start()
+            return 0
+
+        lax.fori_loop(h * 16, h * 16 + 16, store, 0)
+    pltpu.make_async_copy(out, out, store_sem).wait()
 
 
 def body(
@@ -487,10 +485,10 @@
     )
     placed = pl.pallas_call(
         place_kernel,
-        grid=(2,),
         out_shape=jax.ShapeDtypeStruct((4096, 128), F32),
-        in_specs=[pl.BlockSpec((8, 16, 16, 128), lambda n: (0, 0, n, 0))],
-        out_specs=pl.BlockSpec((2048, 128), lambda n: (n, 0)),
+        in_specs=[pl.BlockSpec(memory_space=pltpu.VMEM)],
+        out_specs=pl.BlockSpec(memory_space=pltpu.HBM),
+        scratch_shapes=[pltpu.VMEM((32 * CELL, 128), F32), dma],
         compiler_params=pltpu.CompilerParams(vmem_limit_bytes=16 * 1024 * 1024),
     )(parts)
     return placed.reshape(32, 16, 8, 128)

time: 102 us -> 99.3 us (0.974)
  Pallas kernels: 101 us -> 97.8 us
    pallas_call x1, Pallas kernels: 97.9 us -> 96.3 us  [body(): pl.pallas_call(exchange_kernel, out_shape=jax.ShapeDtypeStruct((8, 16, 32...]
    pallas_call x1, Pallas kernels: 2.89 us -> 1.57 us  [body(): pl.pallas_call(place_kernel, out_shape=jax.ShapeDtypeStruct((4096, 128),...]
where the time goes in v3:
time: 99.3 us; the launch traced here: 99.1 us
  Pallas kernels  97.8 us (98%)
  local copies, waits for them, and re-layouts  1.22 us (1%)
    pallas_call x1, Pallas kernels, body(): pl.pallas_call(exchange_kernel, out_shape=jax.ShapeDtypeStruct((8, 16, 32...  96.3 us

profile of v3, /device:TPU:1, one launch (start us, length us, event | category | flops | bytes accessed | tf_op | source)
XLA Modules:
  0.0 99.1 jit_solution(2303069506662406543)
XLA Ops:
  0.0 96.3 %shard_map.91.parts = bf16[8,16,32,128]{3,2,1,0:T(8,128)(2,1)} custom-call(bf16[4096,128]{1,0:T(8,128)(2,1)} %bitcast.6, bf16[4096,128]{1,0:T(8,128)(2,1)} %bitcast.7, bf16[1024,128]{1,0:T(8,128)(2,1)} %bitcast.8, bf16[1024,128]{1,0:T(8,128)(2,1)} %bitcast.9, s32[512,64]{1,0:T(8,128)} %bitcast.10, bf16[32,1024]{1,0:T(8,128)(2,1)} %t_weights_in.1, ...), custom_call_target="tpu_custom_call" | custom-call | tf_op jit(solution)/shard_map/pallas_call | solution.py:461
  96.3 0.0 copy-start
  96.3 1.2 %copy-done = bf16[8,16,32,128]{3,2,1,0:T(8,128)(2,1)S(1)} copy-done((bf16[8,16,32,128]{3,2,1,0:T(8,128)(2,1)S(1)}, bf16[8,16,32,128]{3,2,1,0:T(8,128)(2,1)}, u32[]{:S(2)}) %copy-start) | copy-done | bytes 1048600
  97.5 1.6 %shard_map.92 = f32[4096,128]{1,0:T(8,128)} custom-call(bf16[8,16,32,128]{3,2,1,0:T(8,128)(2,1)S(1)} %copy-done), custom_call_target="tpu_custom_call" | custom-call | tf_op jit(solution)/shard_map/pallas_call | solution.py:486
Async XLA Ops:
  96.3 1.2 %copy-start = (bf16[8,16,32,128]{3,2,1,0:T(8,128)(2,1)S(1)}, bf16[8,16,32,128]{3,2,1,0:T(8,128)(2,1)}, u32[]{:S(2)}) copy-start(bf16[8,16,32,128]{3,2,1,0:T(8,128)(2,1)} %shard_map.91.parts) | copy-start | bytes 3145732

commit v4 on v3

--- a/solution.py
+++ b/solution.py
@@ -98,7 +98,37 @@
     ]
     for load in loads:
         load.start()
-    for load in loads:
+    for load in loads[:4]:
+        load.wait()
+    pl.semaphore_wait(barrier, 1 + 15 + (SY - 2) + (SX - 1))
+    for k in range(1, SY):
+        signal(ready_y, on_y(k))
+
+    quarter = pl.ds(pl.multiple_of(x * 256, 256), 256)
+
+    def own_rows(m):
+        return pltpu.make_async_copy(
+            rows_own.at[m, :, quarter], time_mats.at[m, block, core, :, quarter], own_sem.at[m]
+        )
+
+    for m in range(2):
+        own_rows(m).start()
+
+        def send_rows(k, _, m=m):
+            remote(
+                rows_own.at[m, :, quarter], time_mats.at[m, block, core, :, quarter],
+                row_send.at[m], row_recv.at[m], in_time(k),
+            )
+            return 0
+
+        lax.fori_loop(1, 16, send_rows, 0)
+
+    own_channels = freq_mats.at[core, x, y // 2]
+    freq_mats[core, x, y // 2] = freq_own[core]
+    for k in range(1, SX):
+        remote(own_channels, own_channels, freq_send.at[0], freq_recv.at[0], on_x(k))
+
+    for load in loads[4:]:
         load.wait()
 
     def spread(t, _):
@@ -149,34 +179,6 @@
         remote(some, some, half_send.at[c], half_recv.at[c], sibling)
 
     update_some(0)
-    pl.semaphore_wait(barrier, 1 + 15 + (SY - 2) + (SX - 1))
-    for k in range(1, SY):
-        signal(ready_y, on_y(k))
-
-    quarter = pl.ds(pl.multiple_of(x * 256, 256), 256)
-
-    def own_rows(m):
-        return pltpu.make_async_copy(
-            rows_own.at[m, :, quarter], time_mats.at[m, block, core, :, quarter], own_sem.at[m]
-        )
-
-    for m in range(2):
-        own_rows(m).start()
-
-        def send_rows(k, _, m=m):
-            remote(
-                rows_own.at[m, :, quarter], time_mats.at[m, block, core, :, quarter],
-                row_send.at[m], row_recv.at[m], in_time(k),
-            )
-            return 0
-
-        lax.fori_loop(1, 16, send_rows, 0)
-
-    own_channels = freq_mats.at[core, x, y // 2]
-    freq_mats[core, x, y // 2] = freq_own[core]
-    for k in range(1, SX):
-        remote(own_channels, own_channels, freq_send.at[0], freq_recv.at[0], on_x(k))
-
     update_some(1)
     send_half(0)
     drain(freq_mats.at[core, pl.ds(0, 3), 0], freq_recv.at[0])

time: 99.3 us -> 96.8 us (0.975)
  Pallas kernels: 97.8 us -> 95.4 us
    pallas_call x1, Pallas kernels: 96.3 us -> 93.8 us  [body(): pl.pallas_call(exchange_kernel, out_shape=jax.ShapeDtypeStruct((8, 16, 32...]
where the time goes in v4:
time: 96.8 us; the launch traced here: 96.6 us
  Pallas kernels  95.4 us (99%)
  local copies, waits for them, and re-layouts  1.22 us (1%)
    pallas_call x1, Pallas kernels, body(): pl.pallas_call(exchange_kernel, out_shape=jax.ShapeDtypeStruct((8, 16, 32...  93.8 us

profile of v4, /device:TPU:1, one launch (start us, length us, event | category | flops | bytes accessed | tf_op | source)
XLA Modules:
  0.0 96.6 jit_solution(581796317206295561)
XLA Ops:
  0.0 93.8 %shard_map.91.parts = bf16[8,16,32,128]{3,2,1,0:T(8,128)(2,1)} custom-call(bf16[4096,128]{1,0:T(8,128)(2,1)} %bitcast.6, bf16[4096,128]{1,0:T(8,128)(2,1)} %bitcast.7, bf16[1024,128]{1,0:T(8,128)(2,1)} %bitcast.8, bf16[1024,128]{1,0:T(8,128)(2,1)} %bitcast.9, s32[512,64]{1,0:T(8,128)} %bitcast.10, bf16[32,1024]{1,0:T(8,128)(2,1)} %t_weights_in.1, ...), custom_call_target="tpu_custom_call" | custom-call | tf_op jit(solution)/shard_map/pallas_call | solution.py:463
  93.8 0.0 copy-start
  93.8 1.2 %copy-done = bf16[8,16,32,128]{3,2,1,0:T(8,128)(2,1)S(1)} copy-done((bf16[8,16,32,128]{3,2,1,0:T(8,128)(2,1)S(1)}, bf16[8,16,32,128]{3,2,1,0:T(8,128)(2,1)}, u32[]{:S(2)}) %copy-start) | copy-done | bytes 1048600
  95.1 1.6 %shard_map.92 = f32[4096,128]{1,0:T(8,128)} custom-call(bf16[8,16,32,128]{3,2,1,0:T(8,128)(2,1)S(1)} %copy-done), custom_call_target="tpu_custom_call" | custom-call | tf_op jit(solution)/shard_map/pallas_call | solution.py:488
Async XLA Ops:
  93.8 1.2 %copy-start = (bf16[8,16,32,128]{3,2,1,0:T(8,128)(2,1)S(1)}, bf16[8,16,32,128]{3,2,1,0:T(8,128)(2,1)}, u32[]{:S(2)}) copy-start(bf16[8,16,32,128]{3,2,1,0:T(8,128)(2,1)} %shard_map.91.parts) | copy-start | bytes 3145732
